TPU v7x, 512 devices: a whole 4x8x8 slice. The times are simulated.
512 devices in a mesh: tile: 128 (over z, y, core), grp: 4 (over x).
Axes of the slice: x: 4, y: 8, z: 8, core: 2. Of those that a mesh axis runs over, the one named last changes fastest.
Arguments:
- kelvin_profile: float32 [90, 128, 256], P(None, 'tile'), may hold values from 0.5 to 1.5
- moisture_profile: float32 [90, 128, 256], P(None, 'tile'), may hold values from 0.1 to 3
- spreading_number: float32 [128, 256], P('tile'), may hold values from 0.05 to 0.24
- overhead_angle_measure: float32 [128, 256], P('tile'), may hold values from 0.2 to 1
- illuminated_mask: int32 [128, 256], P('tile'), may hold values 0 or 1
- radiating_tiles: int32 [32768, 1], P('tile'), may hold values from 0 to 127; in each aligned block of 256 rows (0 to 255, 256 to 511, ...) at most 4 rows name the same one
- cloudy_member_factors: float32 [224, 65536], P('grp', 'tile'), may hold values from 0.25 to 2
- arid_opacity_table: float32 [224, 90], P('grp'), may hold values from 0.003 to 0.2
- moisture_attenuation: float32 [224], P('grp'), may hold values from 0.003 to 0.05
- blackbody_share: float32 [224], P('grp'), may hold values from 0.3 to 3
- insolation_per_quadrature: float32 [224], P('grp'), may hold values from 0.3 to 3
Outputs:
- heating: float32 [90, 128, 256], P(None, 'tile')
- temp_next: float32 [90, 128, 256], P(None, 'tile')
- vapour_next: float32 [90, 128, 256], P(None, 'tile')
Inputs may be any that keep to these rules, and one draw needn't show every extreme that they name: `radiating_tiles`: among the columns of one tile no owner is named more than 4 times, a bound that some block reaches.
All inputs are finite; a program needn't handle non-finite values. No bound on the sum of `illuminated_mask` on one device may be relied on, other than what follows from the above.
Results may differ from a plain program's by a relative error of at most 0.00025.
Values sent between devices are 32-bit elements; how exact they have to be, the bound alone decides.
A program may use at most 64 MiB of HBM per device.

v0:
```python
import math
import jax
import jax.numpy as jnp
from jax import lax
from jax.sharding import PartitionSpec as P

NG = 224


def with_halo(block, sides, width):
    for axis, dim in sides:
        count = lax.axis_size(axis)
        forward = [(i, i + 1) for i in range(count - 1)]
        backward = [(target, source) for source, target in forward]
        low = lax.ppermute(
            lax.slice_in_dim(block, block.shape[dim] - width, None, axis=dim), axis, forward
        )
        high = lax.ppermute(lax.slice_in_dim(block, 0, width, axis=dim), axis, backward)
        block = jnp.concatenate([low, block, high], axis=dim)
    return block


def evaluate_warming(
    kelvin_profile,
    moisture_profile,
    overhead_angle_value,
    illuminated_marker,
    profile_window,
    arid_multiplier,
    moisture_multiplier,
    radiance_share_table,
    sunshine_multiplier,
):
    gpoints, strata_mesh = arid_multiplier.shape
    bundle = math.gcd(gpoints, 4)
    bundles = gpoints // bundle
    lower_mask = (jnp.arange(strata_mesh)[None, :] < jnp.arange(strata_mesh + 1)[:, None]).astype(
        jnp.float32
    )
    upper_mask = 1.0 - lower_mask

    def layer_pass(pieces):
        dry_part, vapour_part, radiance_share_piece, solar_part, sub_part = pieces
        thickness = (
            dry_part[:, :, None]
            + (vapour_part[:, None] * sub_part)[:, None, :] * moisture_profile[None]
        )
        column_depth = jnp.einsum(
            "lk,gkm->glm", lower_mask, thickness, precision=lax.Precision.HIGHEST
        )
        growth = jnp.exp(column_depth)
        damped = jnp.exp(-column_depth)
        infrared_radiance = radiance_share_piece[:, None, None] * kelvin_profile[None]
        downward = damped * jnp.einsum(
            "lk,gkm->glm",
            lower_mask,
            infrared_radiance * growth[:, :strata_mesh] * jnp.expm1(thickness),
            precision=lax.Precision.HIGHEST,
        )
        floor_term = infrared_radiance[:, strata_mesh - 1] * damped[:, strata_mesh]
        upward = growth * (
            floor_term[:, None, :]
            - jnp.einsum(
                "lk,gkm->glm",
                upper_mask,
                infrared_radiance * damped[:, :strata_mesh] * jnp.expm1(-thickness),
                precision=lax.Precision.HIGHEST,
            )
        )
        sunbeam = (
            solar_part[:, None, None]
            * illuminated_marker[None, None, :]
            * jnp.exp(-column_depth / overhead_angle_value[None, None, :])
        )
        fluxes = downward - upward + sunbeam
        return jnp.sum(fluxes[:, :strata_mesh] - fluxes[:, 1:], axis=0)

    spectral = lax.map(
        layer_pass,
        (
            arid_multiplier.reshape(bundles, bundle, strata_mesh),
            moisture_multiplier.reshape(bundles, bundle),
            radiance_share_table.reshape(bundles, bundle),
            sunshine_multiplier.reshape(bundles, bundle),
            profile_window.reshape(bundles, bundle, profile_window.shape[1]),
        ),
    )
    return jnp.sum(spectral, axis=0)


def advance(atmosphere_variables, spreading_number):
    padded = with_halo(atmosphere_variables, (("tile", 2),), 1)
    eastern = jnp.roll(atmosphere_variables, -1, axis=3)
    western = jnp.roll(atmosphere_variables, 1, axis=3)
    return atmosphere_variables + spreading_number * (
        padded[:, :, :-2] + padded[:, :, 2:] + eastern + western - 4.0 * atmosphere_variables
    )


def on_device(
    kelvin_profile,
    moisture_profile,
    spreading_number,
    overhead_angle_measure,
    illuminated_mask,
    radiating_tiles,
    cloudy_member_factors,
    arid_opacity_table,
    moisture_attenuation,
    blackbody_share,
    insolation_per_quadrature,
):
    strata_mesh, parallel_band_sequence, meridian_boxes = kelvin_profile.shape
    atmosphere_variables = jnp.stack([kelvin_profile, moisture_profile])
    for repeat in range(2):
        atmosphere_variables = advance(atmosphere_variables, spreading_number)
    temp_dyn = atmosphere_variables[0]
    vapour_next = atmosphere_variables[1]
    columns = parallel_band_sequence * meridian_boxes
    tile_count = lax.axis_size("tile")
    capacity = cloudy_member_factors.shape[1] // tile_count
    slots = tile_count * capacity
    owner_ids = radiating_tiles[:, 0]
    matches = (owner_ids[:, None] == jnp.arange(tile_count, dtype=jnp.int32)[None, :]).astype(
        jnp.int32
    )
    position = jnp.sum((jnp.cumsum(matches, axis=0) - 1) * matches, axis=1)
    slot_index = owner_ids * capacity + position
    overhead_angle_value = overhead_angle_measure.reshape(columns)
    sunlit_local = overhead_angle_value * illuminated_mask.reshape(columns).astype(jnp.float32)
    column_rows = jnp.concatenate(
        [temp_dyn.reshape(strata_mesh, columns).T, vapour_next.reshape(strata_mesh, columns).T],
        axis=1,
    )
    outgoing = (
        jnp.zeros((slots, 2 * strata_mesh), jnp.float32)
        .at[slot_index]
        .set(column_rows)
        .reshape(tile_count, capacity, 2 * strata_mesh)
    )
    sun_rows = jnp.stack([overhead_angle_value, sunlit_local], axis=1)
    blank = jnp.stack([jnp.ones((slots,), jnp.float32), jnp.zeros((slots,), jnp.float32)], axis=1)
    sun_out = blank.at[slot_index].set(sun_rows).reshape(tile_count, capacity, 2)
    incoming, sun_in = (
        lax.all_to_all(outgoing, "tile", split_axis=0, concat_axis=0, tiled=True),
        lax.all_to_all(sun_out, "tile", split_axis=0, concat_axis=0, tiled=True),
    )
    incoming = incoming.reshape(slots, 2 * strata_mesh)
    sun_in = sun_in.reshape(slots, 2)
    partial_value = evaluate_warming(
        incoming[:, :strata_mesh].T,
        incoming[:, strata_mesh:].T,
        sun_in[:, 0],
        sun_in[:, 1],
        cloudy_member_factors,
        arid_opacity_table,
        moisture_attenuation,
        blackbody_share,
        insolation_per_quadrature,
    )
    summed = lax.psum(partial_value, "grp")
    returning = lax.all_to_all(
        summed.T.reshape(tile_count, capacity, strata_mesh),
        "tile",
        split_axis=0,
        concat_axis=0,
        tiled=True,
    )
    total_heat = returning.reshape(slots, strata_mesh)[slot_index].T
    heating = (total_heat / NG).reshape(strata_mesh, parallel_band_sequence, meridian_boxes)
    return (heating, temp_dyn + heating, vapour_next)


def solution(mesh):
    in_specs = (
        P(None, "tile", None),
        P(None, "tile", None),
        P("tile", None),
        P("tile", None),
        P("tile", None),
        P("tile", None),
        P("grp", "tile"),
        P("grp", None),
        P("grp"),
        P("grp"),
        P("grp"),
    )
    out_specs = (P(None, "tile", None), P(None, "tile", None), P(None, "tile", None))
    return jax.shard_map(
        on_device, mesh=mesh, in_specs=in_specs, out_specs=out_specs, check_vma=False
    )
```

profile of v0, /device:TPU:1, one launch (start us, length us, event | category | flops | bytes accessed | tf_op | source)
XLA Modules:
  0.0 282.9 jit_solution(3957127956137913107)
XLA Ops:
  9.2 8.8 %collective-permute-start.1 = (f32[2,90,1,256]{1,3,2,0:T(8,128)S(1)}, f32[2,90,1,256]{1,3,2,0:T(8,128)S(1)}, u32[]{:S(2)}, u32[]{:S(2)}) collective-permute-start(f32[2,90,1,256]{1,3,2,0:T(8,128)S(1)} %pad_maximum_fusion), channel_id=1, source_target_pairs={{4,0},{8,4},{12,8},{16,12},{20,16},{24,20},{28,24},{32,28},{36,32}... | collective-permute-start | bytes 552968 | tf_op jit(solution)/shard_map/ppermute | solution.py:18
  18.0 1.9 collective-permute-start
  27.0 12.7 %all-to-all-start.1 = ((f32[128,4,2]{1,2,0:T(2,128)}), f32[128,4,2]{1,2,0:T(2,128)S(1)}, u32[]{:S(2)}, u32[]{:S(2)}) async-start(f32[128,4,2]{1,2,0:T(2,128)} %copy.61), calls=%async_computation.1 | async-start | bytes 262144 | tf_op jit(solution)/shard_map/all_to_all | solution.py:146
  39.9 2.8 collective-permute-start.3
  42.7 2.8 collective-permute-start.2
  45.5 2.3 collective-permute-done.3
  48.9 1.7 scatter_custom_fusion
  52.4 15.6 %all-to-all-start = ((f32[128,4,180]{2,1,0:T(4,128)}), f32[128,4,180]{2,1,0:T(4,128)}, u32[]{:S(2)}, u32[]{:S(2)}) async-start(f32[128,4,180]{2,1,0:T(4,128)} %reshape.191), calls=%async_computation | async-start | bytes 1048576 | tf_op jit(solution)/shard_map/all_to_all | solution.py:145
  71.0 1.6 reshape.189
  74.2 14.0 %all-to-all-done = f32[128,4,180]{2,1,0:T(4,128)} async-done(((f32[128,4,180]{2,1,0:T(4,128)}), f32[128,4,180]{2,1,0:T(4,128)}, u32[]{:S(2)}, u32[]{:S(2)}) %all-to-all-start) | async-done | bytes 368672 | tf_op jit(solution)/shard_map/all_to_all | solution.py:145
  88.2 2.0 reshape.192
  90.2 2.0 slice_bitcast_fusion
  94.4 103.7 %while.12 = (s32[]{:T(128)}, f32[14,90,512]{2,1,0:T(8,128)S(1)}, f32[14,4,90]{2,1,0:T(4,128)}, f32[14,4]{1,0:T(8,128)S(1)}, f32[14,4,512]{2,1,0:T(4,128)}, /*ind...) while((s32[]{:T(128)}, f32[14,90,512]{2,1,0:T(8,128)S(1)}, ...), condition=%wide.region_7.8_spmd.clone.clone, body=%wide.region_5.7_spmd.clone.clone.sunk | while | flops 608476160 | bytes 12221821 | solution.py:78
  100.2 1.5 fusion.81
  115.0 1.5 fusion.81
  122.4 1.5 fusion.81
  137.2 1.5 fusion.81
  144.6 1.5 fusion.81
  159.4 1.5 fusion.81
  181.6 1.5 fusion.81
  189.0 1.5 fusion.81
  199.2 42.9 %all-reduce.2.cloned.1.call-done = f32[128,4,90]{2,1,0:T(4,128)} async-done(((f32[128,4,90]{2,1,0:T(4,128)}), f32[128,4,90]{2,1,0:T(4,128)}) %all-reduce.2.cloned.1.call-update) | async-done | bytes 184336 | tf_op jit(solution)/shard_map/psum | solution.py:161
  242.1 16.4 %all-to-all-start.2 = ((f32[128,4,90]{2,1,0:T(4,128)}), f32[128,4,90]{2,1,0:T(4,128)S(1)}, u32[]{:S(2)}, u32[]{:S(2)}) async-start(f32[128,4,90]{2,1,0:T(4,128)} %all-reduce.2.cloned.1.call-done), calls=%async_computation.2 | async-start | bytes 524288 | tf_op jit(solution)/shard_map/all_to_all | solution.py:162
  259.3 14.5 %all-to-all-done.2 = f32[128,4,90]{2,1,0:T(4,128)S(1)} async-done(((f32[128,4,90]{2,1,0:T(4,128)}), f32[128,4,90]{2,1,0:T(4,128)S(1)}, u32[]{:S(2)}, u32[]{:S(2)}) %all-to-all-start.2) | async-done | bytes 184352 | tf_op jit(solution)/shard_map/all_to_all | solution.py:162
  (273 shorter events, 113.1 us)
Async XLA Ops:
  7.2 17.0 %copy-start = (f32[512,2]{1,0:T(8,128)S(1)}, f32[512,2]{1,0:T(8,128)}, u32[]{:S(2)}) copy-start(f32[512,2]{1,0:T(8,128)} %constant.42.clone.1) | copy-start | bytes 12292
  9.2 30.5 %collective-permute-start.1 = (f32[2,90,1,256]{1,3,2,0:T(8,128)S(1)}, f32[2,90,1,256]{1,3,2,0:T(8,128)S(1)}, u32[]{:S(2)}, u32[]{:S(2)}) collective-permute-start(f32[2,90,1,256]{1,3,2,0:T(8,128)S(1)} %pad_maximum_fusion), channel_id=1, source_target_pairs={{4,0},{8,4},{12,8},{16,12},{20,16},{24,20},{28,24},{32,28},{36,32}... | collective-permute-start | bytes 552968 | tf_op jit(solution)/shard_map/ppermute | solution.py:18
  18.0 21.7 %collective-permute-start = (f32[2,90,1,256]{1,3,2,0:T(8,128)S(1)}, f32[2,90,1,256]{1,3,2,0:T(8,128)S(1)}, u32[]{:S(2)}, u32[]{:S(2)}) collective-permute-start(f32[2,90,1,256]{1,3,2,0:T(8,128)S(1)} %pad_maximum_fusion), channel_id=1, source_target_pairs={{0,4},{4,8},{8,12},{12,16},{16,20},{20,24},{24,28},{28,32},{32,36}... | collective-permute-start | bytes 552968 | tf_op jit(solution)/shard_map/ppermute | solution.py:15
  20.7 19.0 %copy-start.2 = (f32[1,256]{1,0:T(1,128)S(1)}, f32[1,256]{1,0:T(1,128)}, u32[]{:S(2)}) copy-start(f32[1,256]{1,0:T(1,128)} %param.15) | copy-start | bytes 3076
  27.0 25.5 %all-to-all-start.1 = ((f32[128,4,2]{1,2,0:T(2,128)}), f32[128,4,2]{1,2,0:T(2,128)S(1)}, u32[]{:S(2)}, u32[]{:S(2)}) async-start(f32[128,4,2]{1,2,0:T(2,128)} %copy.61), calls=%async_computation.1 | async-start | bytes 262144 | tf_op jit(solution)/shard_map/all_to_all | solution.py:146
  39.9 8.0 %collective-permute-start.3 = (f32[2,90,1,256]{1,3,2,0:T(8,128)S(1)}, f32[2,90,1,256]{1,3,2,0:T(8,128)S(1)}, u32[]{:S(2)}, u32[]{:S(2)}) collective-permute-start(f32[2,90,1,256]{1,3,2,0:T(8,128)S(1)} %fusion.45), channel_id=1, source_target_pairs={{4,0},{8,4},{12,8},{16,12},{20,16},{24,20},{28,24},{32,28},{36,32}... | collective-permute-start | bytes 552968 | tf_op jit(solution)/shard_map/ppermute | solution.py:18
  42.7 6.1 %collective-permute-start.2 = (f32[2,90,1,256]{1,3,2,0:T(8,128)S(1)}, f32[2,90,1,256]{1,3,2,0:T(8,128)S(1)}, u32[]{:S(2)}, u32[]{:S(2)}) collective-permute-start(f32[2,90,1,256]{1,3,2,0:T(8,128)S(1)} %fusion.45), channel_id=1, source_target_pairs={{0,4},{4,8},{8,12},{12,16},{16,20},{20,24},{24,28},{28,32},{32,36}... | collective-permute-start | bytes 552968 | tf_op jit(solution)/shard_map/ppermute | solution.py:15
  45.5 22.7 %copy-start.4 = (f32[56]{0:T(128)S(1)}, f32[56]{0:T(128)}, u32[]{:S(2)}) copy-start(f32[56]{0:T(128)} %param.21) | copy-start | bytes 676
  52.4 15.6 %copy-start.1 = (f32[128,4,2]{1,2,0:T(2,128)}, f32[128,4,2]{1,2,0:T(2,128)S(1)}, u32[]{:S(2)}) copy-start(f32[128,4,2]{1,2,0:T(2,128)S(1)} %all-to-all-done.1) | copy-start | bytes 12292
  52.4 35.8 %all-to-all-start = ((f32[128,4,180]{2,1,0:T(4,128)}), f32[128,4,180]{2,1,0:T(4,128)}, u32[]{:S(2)}, u32[]{:S(2)}) async-start(f32[128,4,180]{2,1,0:T(4,128)} %reshape.191), calls=%async_computation | async-start | bytes 1048576 | tf_op jit(solution)/shard_map/all_to_all | solution.py:145
  68.0 174.1 %all-reduce.2.cloned.1.call-start = ((), (), s32[]{:S(2)}) async-start(), calls=%async_computation.3 | async-start | bytes 524288 | tf_op jit(solution)/shard_map/psum | solution.py:161
  98.4 1.7 copy-start.3
  105.9 1.7 copy-start.3
  113.3 1.7 copy-start.3
  120.7 1.7 copy-start.3
  128.1 1.7 copy-start.3
  135.5 1.7 copy-start.3
  142.9 1.7 copy-start.3
  150.3 1.7 copy-start.3
  157.7 1.7 copy-start.3
  172.5 1.7 copy-start.3
  179.9 1.7 copy-start.3
  194.7 1.7 copy-start.3
  242.1 31.7 %all-to-all-start.2 = ((f32[128,4,90]{2,1,0:T(4,128)}), f32[128,4,90]{2,1,0:T(4,128)S(1)}, u32[]{:S(2)}, u32[]{:S(2)}) async-start(f32[128,4,90]{2,1,0:T(4,128)} %all-reduce.2.cloned.1.call-done), calls=%async_computation.2 | async-start | bytes 524288 | tf_op jit(solution)/shard_map/all_to_all | solution.py:162
  (2 other events, 3.4 us)
Sparse Core Ops, SparseCore 0:
  199.4 42.6 all-reduce.1
where the time goes:
time: 286 us; the launch traced here: 283 us
  waiting for transfers between devices  75.5 us (26%)
  starting transfers between devices  61.2 us (21%)
  matrix products  54.1 us (19%)
  local copies, waits for them, and re-layouts  52.1 us (18%)
  other arithmetic  24.2 us (8%)
  between operations  14.3 us (5%)
    psum x1, waiting for transfers between devices, on_device(): summed = lax.psum(partial_value, 'grp')  42.9 us
    dot_general x14, matrix products, layer_pass(): jnp.einsum('lk,gkm->glm', lower_mask, infrared_radiance * growth[:, :stra...  21.2 us
    dot_general x14, matrix products, layer_pass(): jnp.einsum('lk,gkm->glm', upper_mask, infrared_radiance * damped[:, :stra...  19.8 us
    all_to_all x1, starting transfers between devices, on_device(): lax.all_to_all(summed.T.reshape(tile_count, capacity, strata_mesh), 'tile...  16.4 us
    all_to_all x1, starting transfers between devices, on_device(): lax.all_to_all(outgoing, 'tile', split_axis=0, concat_axis=0, tiled=True)  15.6 us
    all_to_all x1, waiting for transfers between devices, on_device(): lax.all_to_all(summed.T.reshape(tile_count, capacity, strata_mesh), 'tile...  14.5 us
    all_to_all x1, waiting for transfers between devices, on_device(): lax.all_to_all(outgoing, 'tile', split_axis=0, concat_axis=0, tiled=True)  14 us
    dot_general x14, matrix products, layer_pass(): jnp.einsum('lk,gkm->glm', lower_mask, thickness, precision=lax.Precision....  13.1 us
  transfers between devices with their start and end apart: 8, of which 6 were waited for; matrix products, arithmetic and copies ran while one was open for 6% of the time, Pallas kernels for 0%

commit v1 on v0

--- a/solution.py
+++ b/solution.py
@@ -110,6 +110,12 @@
     blackbody_share,
     insolation_per_quadrature,
 ):
+
+    def threads_shape(m):
+        kept_arr = lax.all_gather(m, "grp")
+        z2 = jnp.sum(kept_arr, axis=0)
+        return z2
+
     strata_mesh, parallel_band_sequence, meridian_boxes = kelvin_profile.shape
     atmosphere_variables = jnp.stack([kelvin_profile, moisture_profile])
     for repeat in range(2):
@@ -158,7 +164,7 @@
         blackbody_share,
         insolation_per_quadrature,
     )
-    summed = lax.psum(partial_value, "grp")
+    summed = threads_shape(partial_value)
     returning = lax.all_to_all(
         summed.T.reshape(tile_count, capacity, strata_mesh),
         "tile",

time: 286 us -> 234 us (0.82)
  waiting for transfers between devices: 75.5 us -> 32.9 us
  between operations: 14.3 us -> 0.92 us
  blocking collectives: 0 us -> 13.1 us
  starting transfers between devices: 61.2 us -> 51.1 us
    psum x1 -> x0, waiting for transfers between devices: 42.9 us -> none  [on_device(): summed = lax.psum(partial_value, 'grp')]
    all_gather x0 -> x1, blocking collectives: none -> 13.1 us  [threads_shape(): kept_arr = lax.all_gather(m, 'grp')]
    all_to_all x1, starting transfers between devices: 16.4 us -> 6.54 us  [on_device(): lax.all_to_all(summed.T.reshape(tile_count, capacity, strata_mesh), 'tile...]
  transfers between devices with their start and end apart: 8 -> 7, of which waited for: 6 -> 5; matrix products, arithmetic and copies ran while one was open for 6% -> 7% of each run, Pallas kernels for 0% -> 0%
where the time goes in v1:
time: 234 us; the launch traced here: 231 us
  matrix products  54.1 us (23%)
  local copies, waits for them, and re-layouts  52.7 us (23%)
  starting transfers between devices  51.1 us (22%)
  waiting for transfers between devices  32.9 us (14%)
  other arithmetic  25 us (11%)
  blocking collectives  13.1 us (6%)
    dot_general x14, matrix products, layer_pass(): jnp.einsum('lk,gkm->glm', lower_mask, infrared_radiance * growth[:, :stra...  21.2 us
    dot_general x14, matrix products, layer_pass(): jnp.einsum('lk,gkm->glm', upper_mask, infrared_radiance * damped[:, :stra...  19.8 us
    all_to_all x1, starting transfers between devices, on_device(): lax.all_to_all(outgoing, 'tile', split_axis=0, concat_axis=0, tiled=True)  15.6 us
    all_to_all x1, waiting for transfers between devices, on_device(): lax.all_to_all(summed.T.reshape(tile_count, capacity, strata_mesh), 'tile...  14.6 us
    all_to_all x1, waiting for transfers between devices, on_device(): lax.all_to_all(outgoing, 'tile', split_axis=0, concat_axis=0, tiled=True)  14.2 us
    dot_general x14, matrix products, layer_pass(): jnp.einsum('lk,gkm->glm', lower_mask, thickness, precision=lax.Precision....  13.1 us
    all_gather x1, blocking collectives, threads_shape(): kept_arr = lax.all_gather(m, 'grp')  13.1 us
    all_to_all x1, starting transfers between devices, on_device(): lax.all_to_all(sun_out, 'tile', split_axis=0, concat_axis=0, tiled=True)  12.7 us
  transfers between devices with their start and end apart: 7, of which 5 were waited for; matrix products, arithmetic and copies ran while one was open for 7% of the time, Pallas kernels for 0%

profile of v1, /device:TPU:1, one launch (start us, length us, event | category | flops | bytes accessed | tf_op | source)
XLA Modules:
  0.0 231.3 jit_solution(12192240066263403781)
XLA Ops:
  2.7 8.8 %collective-permute-start.1 = (f32[2,90,1,256]{1,3,2,0:T(8,128)S(1)}, f32[2,90,1,256]{1,3,2,0:T(8,128)S(1)}, u32[]{:S(2)}, u32[]{:S(2)}) collective-permute-start(f32[2,90,1,256]{1,3,2,0:T(8,128)S(1)} %pad_maximum_fusion), channel_id=1, source_target_pairs={{4,0},{8,4},{12,8},{16,12},{20,16},{24,20},{28,24},{32,28},{36,32}... | collective-permute-start | bytes 552968 | tf_op jit(solution)/shard_map/ppermute | solution.py:18
  11.5 1.9 collective-permute-start
  20.4 12.7 %all-to-all-start.1 = ((f32[128,4,2]{1,2,0:T(2,128)}), f32[128,4,2]{1,2,0:T(2,128)S(1)}, u32[]{:S(2)}, u32[]{:S(2)}) async-start(f32[128,4,2]{1,2,0:T(2,128)} %copy.74), calls=%async_computation.1 | async-start | bytes 262144 | tf_op jit(solution)/shard_map/all_to_all | solution.py:152
  33.4 2.8 %collective-permute-start.3 = (f32[2,90,1,256]{1,3,2,0:T(8,128)S(1)}, f32[2,90,1,256]{1,3,2,0:T(8,128)S(1)}, u32[]{:S(2)}, u32[]{:S(2)}) collective-permute-start(f32[2,90,1,256]{1,3,2,0:T(8,128)S(1)} %fusion.45), channel_id=1, source_target_pairs={{4,0},{8,4},{12,8},{16,12},{20,16},{24,20},{28,24},{32,28},{36,32}... | collective-permute-start | bytes 552968 | tf_op jit(solution)/shard_map/ppermute | solution.py:18
  36.2 2.8 %collective-permute-start.2 = (f32[2,90,1,256]{1,3,2,0:T(8,128)S(1)}, f32[2,90,1,256]{1,3,2,0:T(8,128)S(1)}, u32[]{:S(2)}, u32[]{:S(2)}) collective-permute-start(f32[2,90,1,256]{1,3,2,0:T(8,128)S(1)} %fusion.45), channel_id=1, source_target_pairs={{0,4},{4,8},{8,12},{12,16},{16,20},{20,24},{24,28},{28,32},{32,36}... | collective-permute-start | bytes 552968 | tf_op jit(solution)/shard_map/ppermute | solution.py:15
  39.0 2.3 %collective-permute-done.3 = f32[2,90,1,256]{1,3,2,0:T(8,128)S(1)} collective-permute-done((f32[2,90,1,256]{1,3,2,0:T(8,128)S(1)}, f32[2,90,1,256]{1,3,2,0:T(8,128)S(1)}, u32[]{:S(2)}, u32[]{:S(2)}) %collective-permute-start.3) | collective-permute-done | bytes 184352 | tf_op jit(solution)/shard_map/ppermute | solution.py:18
  42.4 1.7 scatter_custom_fusion
  46.5 15.6 %all-to-all-start = ((f32[128,4,180]{2,1,0:T(4,128)}), f32[128,4,180]{2,1,0:T(4,128)}, u32[]{:S(2)}, u32[]{:S(2)}) async-start(f32[128,4,180]{2,1,0:T(4,128)} %reshape.191), calls=%async_computation | async-start | bytes 1048576 | tf_op jit(solution)/shard_map/all_to_all | solution.py:151
  64.9 1.6 reshape.189
  68.1 14.2 %all-to-all-done = f32[128,4,180]{2,1,0:T(4,128)} async-done(((f32[128,4,180]{2,1,0:T(4,128)}), f32[128,4,180]{2,1,0:T(4,128)}, u32[]{:S(2)}, u32[]{:S(2)}) %all-to-all-start) | async-done | bytes 368672 | tf_op jit(solution)/shard_map/all_to_all | solution.py:151
  82.3 2.0 reshape.192
  84.3 2.0 slice_bitcast_fusion
  88.5 103.7 %while.12 = (s32[]{:T(128)}, f32[14,90,512]{2,1,0:T(8,128)S(1)}, f32[14,4,90]{2,1,0:T(4,128)}, f32[14,4]{1,0:T(8,128)S(1)}, f32[14,4,512]{2,1,0:T(4,128)}, /*ind...) while((s32[]{:T(128)}, f32[14,90,512]{2,1,0:T(8,128)S(1)}, ...), condition=%wide.region_7.8_spmd.clone.clone, body=%wide.region_5.7_spmd.clone.clone.sunk | while | flops 608476160 | bytes 12221821 | solution.py:78
  94.3 1.5 fusion.81
  101.7 1.5 fusion.81
  116.5 1.5 fusion.81
  123.9 1.5 fusion.81
  138.7 1.5 fusion.81
  146.1 1.5 fusion.81
  160.9 1.5 fusion.81
  183.1 1.5 fusion.81
  193.1 13.1 %all-gather.1 = f32[4,90,512]{2,1,0:T(8,128)S(1)} all-gather(f32[1,90,512]{2,1,0:T(8,128)} %bitcast.145), channel_id=2, replica_groups=mesh['tile'=128,'grp'=4] {'grp'}, dimensions={0}, use_global_device_ids=true | all-gather | bytes 921600 | tf_op jit(solution)/shard_map/all_gather | solution.py:115
  207.1 6.5 %all-to-all-start.2 = ((f32[128,4,90]{2,1,0:T(4,128)}), f32[128,4,90]{2,1,0:T(4,128)S(1)}, u32[]{:S(2)}, u32[]{:S(2)}) async-start(f32[128,4,90]{2,1,0:T(4,128)} %bitcast.22), calls=%async_computation.2 | async-start | bytes 524288 | tf_op jit(solution)/shard_map/all_to_all | solution.py:168
  214.4 14.6 %all-to-all-done.2 = f32[128,4,90]{2,1,0:T(4,128)S(1)} async-done(((f32[128,4,90]{2,1,0:T(4,128)}), f32[128,4,90]{2,1,0:T(4,128)S(1)}, u32[]{:S(2)}, u32[]{:S(2)}) %all-to-all-start.2) | async-done | bytes 184352 | tf_op jit(solution)/shard_map/all_to_all | solution.py:168
  (272 shorter events, 114.2 us)
Async XLA Ops:
  0.6 17.0 %copy-start = (f32[512,2]{1,0:T(8,128)S(1)}, f32[512,2]{1,0:T(8,128)}, u32[]{:S(2)}) copy-start(f32[512,2]{1,0:T(8,128)} %constant.42.clone.1) | copy-start | bytes 12292
  2.7 30.5 %collective-permute-start.1 = (f32[2,90,1,256]{1,3,2,0:T(8,128)S(1)}, f32[2,90,1,256]{1,3,2,0:T(8,128)S(1)}, u32[]{:S(2)}, u32[]{:S(2)}) collective-permute-start(f32[2,90,1,256]{1,3,2,0:T(8,128)S(1)} %pad_maximum_fusion), channel_id=1, source_target_pairs={{4,0},{8,4},{12,8},{16,12},{20,16},{24,20},{28,24},{32,28},{36,32}... | collective-permute-start | bytes 552968 | tf_op jit(solution)/shard_map/ppermute | solution.py:18
  11.5 21.7 %collective-permute-start = (f32[2,90,1,256]{1,3,2,0:T(8,128)S(1)}, f32[2,90,1,256]{1,3,2,0:T(8,128)S(1)}, u32[]{:S(2)}, u32[]{:S(2)}) collective-permute-start(f32[2,90,1,256]{1,3,2,0:T(8,128)S(1)} %pad_maximum_fusion), channel_id=1, source_target_pairs={{0,4},{4,8},{8,12},{12,16},{16,20},{20,24},{24,28},{28,32},{32,36}... | collective-permute-start | bytes 552968 | tf_op jit(solution)/shard_map/ppermute | solution.py:15
  14.2 19.0 %copy-start.2 = (f32[1,256]{1,0:T(1,128)S(1)}, f32[1,256]{1,0:T(1,128)}, u32[]{:S(2)}) copy-start(f32[1,256]{1,0:T(1,128)} %param.15) | copy-start | bytes 3076
  20.4 25.5 %all-to-all-start.1 = ((f32[128,4,2]{1,2,0:T(2,128)}), f32[128,4,2]{1,2,0:T(2,128)S(1)}, u32[]{:S(2)}, u32[]{:S(2)}) async-start(f32[128,4,2]{1,2,0:T(2,128)} %copy.74), calls=%async_computation.1 | async-start | bytes 262144 | tf_op jit(solution)/shard_map/all_to_all | solution.py:152
  33.4 8.0 %collective-permute-start.3 = (f32[2,90,1,256]{1,3,2,0:T(8,128)S(1)}, f32[2,90,1,256]{1,3,2,0:T(8,128)S(1)}, u32[]{:S(2)}, u32[]{:S(2)}) collective-permute-start(f32[2,90,1,256]{1,3,2,0:T(8,128)S(1)} %fusion.45), channel_id=1, source_target_pairs={{4,0},{8,4},{12,8},{16,12},{20,16},{24,20},{28,24},{32,28},{36,32}... | collective-permute-start | bytes 552968 | tf_op jit(solution)/shard_map/ppermute | solution.py:18
  36.2 6.1 %collective-permute-start.2 = (f32[2,90,1,256]{1,3,2,0:T(8,128)S(1)}, f32[2,90,1,256]{1,3,2,0:T(8,128)S(1)}, u32[]{:S(2)}, u32[]{:S(2)}) collective-permute-start(f32[2,90,1,256]{1,3,2,0:T(8,128)S(1)} %fusion.45), channel_id=1, source_target_pairs={{0,4},{4,8},{8,12},{12,16},{16,20},{20,24},{24,28},{28,32},{32,36}... | collective-permute-start | bytes 552968 | tf_op jit(solution)/shard_map/ppermute | solution.py:15
  39.0 23.2 %copy-start.4 = (f32[56]{0:T(128)S(1)}, f32[56]{0:T(128)}, u32[]{:S(2)}) copy-start(f32[56]{0:T(128)} %param.21) | copy-start | bytes 676
  46.5 35.8 %all-to-all-start = ((f32[128,4,180]{2,1,0:T(4,128)}), f32[128,4,180]{2,1,0:T(4,128)}, u32[]{:S(2)}, u32[]{:S(2)}) async-start(f32[128,4,180]{2,1,0:T(4,128)} %reshape.191), calls=%async_computation | async-start | bytes 1048576 | tf_op jit(solution)/shard_map/all_to_all | solution.py:151
  92.5 1.7 copy-start.3
  99.9 1.7 copy-start.3
  107.3 1.7 copy-start.3
  114.8 1.7 copy-start.3
  122.2 1.7 copy-start.3
  129.6 1.7 copy-start.3
  137.0 1.7 copy-start.3
  144.4 1.7 copy-start.3
  151.8 1.7 copy-start.3
  159.2 1.7 copy-start.3
  166.6 1.7 copy-start.3
  174.0 1.7 copy-start.3
  181.4 1.7 copy-start.3
  188.8 1.7 copy-start.3
  207.1 21.9 %all-to-all-start.2 = ((f32[128,4,90]{2,1,0:T(4,128)}), f32[128,4,90]{2,1,0:T(4,128)S(1)}, u32[]{:S(2)}, u32[]{:S(2)}) async-start(f32[128,4,90]{2,1,0:T(4,128)} %bitcast.22), calls=%async_computation.2 | async-start | bytes 524288 | tf_op jit(solution)/shard_map/all_to_all | solution.py:168
  (1 other events, 0.6 us)
